TPU v7x, 256 devices: a whole 4x4x8 slice. The times are simulated.
256 devices in a mesh: ctx: 32 (over x, z), cls: 8 (over y, core).
Axes of the slice: x: 4, y: 4, z: 8, core: 2. Of those that a mesh axis runs over, the one named last changes fastest.
Arguments:
- tokens: bfloat16 [196608, 8192], P(('ctx', 'cls')), may hold values from -80 to 80
- doc_length: int32 [1], replicated, may hold values from 98304 to 196608
- queries: bfloat16 [64, 8192], P('cls', 'ctx'), may hold values from -0.046875 to 0.046875
- norm_gain: float32 [8192], P('ctx'), may hold values from 0.1 to 1.9
- head_weight: bfloat16 [8192, 4096], P('ctx', 'cls'), may hold values from -0.0625 to 0.0625
- head_bias: float32 [4096], P('cls'), may hold values from -20 to 20
- labels: int32 [4096], P('cls'), may hold values 0 or 1
Outputs:
- mean_loss: float32 [], replicated
- query_grad: float32 [64, 8192], P('cls', 'ctx')
- head_grad: float32 [8192, 4096], P('ctx', 'cls')
- bias_grad: float32 [4096], P('cls')
All inputs are finite; a program needn't handle non-finite values. No bound on the sum of `labels` on one device may be relied on, other than what follows from the above.
Results may differ from a plain program's by a relative error of at most 0.017.
Values may be sent and summed in bfloat16 or wider, within the bound.
A program may use at most 64 MiB of HBM per device.

v0:
```python
import jax
import jax.numpy as jnp
from jax import lax
from jax.sharding import PartitionSpec as P


def shards(tokens, doc_length, queries, norm_gain, head_weight, head_bias, labels):
    context_count = lax.axis_size("ctx")
    class_count = lax.axis_size("cls")
    context_index = lax.axis_index("ctx")
    class_index = lax.axis_index("cls")
    token_count = tokens.shape[0]
    query_share = queries.shape[0]
    width_share = queries.shape[1]
    full_width = width_share * context_count

    def project_add(block_piece):
        return lax.dot_general(
            block_piece, tokens, (((1,), (1,)), ((), ())), preferred_element_type=jnp.float32
        )

    query_block = lax.all_gather(queries, "cls", axis=0, tiled=True)
    scores = project_add(lax.all_gather(query_block, "ctx", axis=1, tiled=True))
    offset = (context_index * class_count + class_index) * token_count
    position = offset + jnp.arange(token_count, dtype=jnp.int32)
    valid_mask = (position < doc_length[0])[None, :]
    local_peak = jnp.max(jnp.where(valid_mask, scores, -1e30), axis=1)
    peak = lax.pmax(local_peak, ("ctx", "cls"))
    weights = jnp.exp(jnp.where(valid_mask, scores - peak[:, None], -1e30))
    pooled_part = jnp.dot(weights.astype(jnp.bfloat16), tokens, preferred_element_type=jnp.float32)
    whole_sum = lax.psum(pooled_part, ("ctx", "cls"))
    pooled = lax.dynamic_slice(
        whole_sum,
        (class_index * query_share, context_index * width_share),
        (query_share, width_share),
    )
    scaled_b = (pooled * norm_gain[None, :]).astype(jnp.bfloat16)
    head_blocks = head_weight.reshape(width_share, query_share, -1)
    square_part = jnp.sum(pooled * pooled, axis=1)
    logit_part = jnp.einsum("hd,dha->ha", scaled_b, head_blocks, preferred_element_type=jnp.float32)
    squares, logit_raw = lax.psum((square_part, logit_part), "ctx")
    inverse_rms = lax.rsqrt(squares / full_width + 1e-05)
    logits = inverse_rms[:, None] * logit_raw + head_bias.reshape(query_share, -1)
    target = labels.reshape(query_share, -1).astype(jnp.float32)
    loss_part = jnp.sum(jax.nn.softplus(logits) - target * logits)
    mean_loss = lax.psum(loss_part, "cls") / (labels.shape[0] * class_count)
    logit_grad = jax.nn.sigmoid(logits) - target
    normed = pooled * inverse_rms[:, None] * norm_gain[None, :]
    head_grad = jnp.einsum("hd,ha->dha", normed, logit_grad).reshape(width_share, -1)
    normed_grad = (
        jnp.einsum("dha,ha->hd", head_blocks.astype(jnp.float32), logit_grad) * norm_gain[None, :]
    )
    unit_pooled = pooled * inverse_rms[:, None]
    inner_part = jnp.sum(unit_pooled * normed_grad, axis=1)
    inner_mean = lax.psum(inner_part, "ctx") / full_width
    pooled_grad = (inverse_rms[:, None] * (normed_grad - unit_pooled * inner_mean[:, None])).astype(
        jnp.bfloat16
    )
    grad_block = lax.all_gather(pooled_grad, "cls", axis=0, tiled=True)
    projected = project_add(lax.all_gather(grad_block, "ctx", axis=1, tiled=True))
    score_grad = (weights * projected).astype(jnp.bfloat16)
    query_part = jnp.dot(score_grad, tokens, preferred_element_type=jnp.float32)
    column_grad = lax.psum_scatter(query_part, "ctx", scatter_dimension=1, tiled=True)
    query_grad = lax.psum_scatter(column_grad, "cls", scatter_dimension=0, tiled=True)
    return (mean_loss, query_grad, head_grad, logit_grad.reshape(-1))


def solution(mesh):
    return jax.shard_map(
        shards,
        mesh=mesh,
        in_specs=(
            P(("ctx", "cls"), None),
            P(),
            P("cls", "ctx"),
            P("ctx"),
            P("ctx", "cls"),
            P("cls"),
            P("cls"),
        ),
        out_specs=(P(), P("cls", "ctx"), P("ctx", "cls"), P("cls")),
        check_vma=False,
    )
```

profile of v0, /device:TPU:2, one launch (start us, length us, event | category | flops | bytes accessed | tf_op | source)
XLA Modules:
  0.0 943.6 jit_solution(2797138843445842792)
XLA Ops:
  7.2 14.3 %all_gather.12 = bf16[64,256]{1,0:T(8,128)(2,1)} all-gather(bf16[8,256]{1,0:T(8,128)(2,1)} %param.9), channel_id=1, replica_groups=mesh['ctx'=32,'cls'=8] {'cls'}, dimensions={0}, use_global_device_ids=true | all-gather | bytes 36864 | tf_op jit(solution)/shard_map/all_gather | solution.py:22
  22.3 72.8 %all-gather.3.cloned.1.call-done = bf16[64,8192]{1,0:T(8,128)(2,1)} async-done(((bf16[64,256]{1,0:T(8,128)(2,1)}), bf16[64,8192]{1,0:T(8,128)(2,1)}) %all-gather.3.cloned.1.call-update) | async-done | bytes 1048592 | tf_op jit(solution)/shard_map/all_gather | solution.py:23
  95.0 8.9 select_reduce_fusion
  104.0 74.6 %pmax.7 = f32[64]{0:T(128)S(1)} all-reduce(f32[64]{0:T(128)S(1)} %get-tuple-element.16), channel_id=1, replica_groups=mesh['ctx'=32,'cls'=8] {'ctx','cls'}, use_global_device_ids=true, to_apply=%region_1.2 | all-reduce | flops 64 | bytes 512 | tf_op jit(solution)/shard_map/pmax | solution.py:28
  178.6 8.2 fusion.3
  187.0 0.1 copy.12
  187.3 257.2 %all-reduce.3.cloned.1.call-done = f32[64,8192]{1,0:T(8,128)} async-done(((f32[64,8192]{1,0:T(8,128)}), f32[64,8192]{1,0:T(8,128)}) %all-reduce.3.cloned.1.call-update) | async-done | bytes 2097168 | tf_op jit(solution)/shard_map/psum | solution.py:31
  444.5 0.8 multiply_reduce_fusion.1
  445.3 0.2 fusion.11
  445.5 61.5 %all-reduce = (f32[8,64]{1,0:T(8,128)S(1)}, f32[8]{0:T(128)S(1)}) all-reduce(f32[8,64]{1,0:T(8,128)S(1)} %bitcast.32, f32[8]{0:T(128)S(1)} %get-tuple-element.12), channel_id=1, replica_groups=mesh['ctx'=32,'cls'=8] {'ctx'}, use_global_device_ids=true, to_apply=%region_5.6 | all-reduce | flops 520 | bytes 4160 | tf_op jit(solution)/shard_map/psum | solution.py:41
  507.0 0.7 divide_subtract_fusion
  507.7 0.1 fusion.18
  507.8 0.9 multiply_multiply_fusion
  508.7 69.2 %psum.39 = f32[8]{0:T(128)S(1)} all-reduce(f32[8]{0:T(128)S(1)} %get-tuple-element.11), channel_id=1, replica_groups=mesh['ctx'=32,'cls'=8] {'ctx'}, use_global_device_ids=true, to_apply=%region_9.10 | all-reduce | flops 8 | bytes 64 | tf_op jit(solution)/shard_map/psum | solution.py:55
  577.9 0.8 multiply_convert_fusion
  578.7 13.7 %all_gather.14 = bf16[64,256]{1,0:T(8,128)(2,1)} all-gather(bf16[8,256]{1,0:T(8,128)(2,1)S(1)} %multiply_convert_fusion), channel_id=1, replica_groups=mesh['ctx'=32,'cls'=8] {'cls'}, dimensions={0}, use_global_device_ids=true | all-gather | bytes 36864 | tf_op jit(solution)/shard_map/all_gather | solution.py:59
  592.4 0.2 reduce-scatter.3.cloned.1.call-start
  592.6 76.7 %all-gather.5.cloned.1.call-done = bf16[64,8192]{1,0:T(8,128)(2,1)} async-done(((bf16[64,256]{1,0:T(8,128)(2,1)}), bf16[64,8192]{1,0:T(8,128)(2,1)}) %all-gather.5.cloned.1.call-update) | async-done | bytes 1048592 | tf_op jit(solution)/shard_map/all_gather | solution.py:60
  669.4 17.7 %fusion.1 = f32[64,8192]{1,0:T(8,128)} fusion(bf16[768,8192]{1,0:T(8,128)(2,1)} %param.7, bf16[64,8192]{1,0:T(8,128)(2,1)} %all-gather.5.cloned.1.call-done, f32[64,768]{1,0:T(8,128)S(1)} %get-tuple-element.17, f32[64]{0:T(128)S(1)} %pmax.7, pred[768]{0:T(1024)(128)(4,1)S(1)} %add_compare_fusion), kind=kOutput, calls=%fused_computation.2 | convolution fusion | flops 1610809344 | bytes 15926272 | tf_op jit(solution)/shard_map/dot_general | solution.py:62
  687.2 13.1 %psum.38 = f32[]{:T(128)} all-reduce(f32[]{:T(128)} %get-tuple-element.15), channel_id=1, replica_groups=mesh['ctx'=32,'cls'=8] {'cls'}, use_global_device_ids=true, to_apply=%region_7.8 | all-reduce | flops 1 | bytes 8 | tf_op jit(solution)/shard_map/psum | solution.py:46
  700.2 0.7 reshape.34
  700.9 200.1 %reduce-scatter.3.cloned.1.call-done = f32[64,256]{1,0:T(8,128)} async-done(((f32[64,8192]{1,0:T(8,128)}), f32[64,256]{1,0:T(8,128)}) %reduce-scatter.3.cloned.1.call-update) | async-done | bytes 65552 | tf_op jit(solution)/shard_map/reduce_scatter | solution.py:63
  901.1 1.0 copy.13
  902.8 33.2 %reduce-scatter.5.cloned.1.call-done = f32[8,256]{1,0:T(8,128)} async-done(((f32[64,256]{1,0:T(8,128)}), f32[8,256]{1,0:T(8,128)}) %reduce-scatter.5.cloned.1.call-update) | async-done | bytes 8208 | tf_op jit(solution)/shard_map/reduce_scatter | solution.py:64
  (24 shorter events, 0.6 us)
Async XLA Ops:
  7.2 87.9 %all-gather.3.cloned.1.call-start = ((), (), s32[]{:S(2)}) async-start(), calls=%async_computation.2 | async-start | bytes 1081344 | tf_op jit(solution)/shard_map/all_gather | solution.py:23
  21.6 422.9 %all-reduce.3.cloned.1.call-start = ((), (), s32[]{:S(2)}) async-start(), calls=%async_computation.3 | async-start | bytes 4194304 | tf_op jit(solution)/shard_map/psum | solution.py:31
  104.0 83.0 %copy-start = (bf16[256,512]{1,0:T(8,128)(2,1)S(1)}, bf16[256,512]{1,0:T(8,128)(2,1)}, u32[]{:S(2)}) copy-start(bf16[256,512]{1,0:T(8,128)(2,1)} %param.11) | copy-start | bytes 786436
  104.0 83.1 %copy-start.3 = (s32[512]{0:T(512)S(1)}, s32[512]{0:T(512)}, u32[]{:S(2)}) copy-start(s32[512]{0:T(512)} %param.13) | copy-start | bytes 6148
  104.0 83.2 %copy-start.2 = (f32[512]{0:T(512)S(1)}, f32[512]{0:T(512)}, u32[]{:S(2)}) copy-start(f32[512]{0:T(512)} %param.12) | copy-start | bytes 6148
  104.0 340.5 %copy-start.1 = (f32[256]{0:T(256)S(1)}, f32[256]{0:T(256)}, u32[]{:S(2)}) copy-start(f32[256]{0:T(256)} %param.10) | copy-start | bytes 3076
  186.9 482.5 %all-gather.5.cloned.1.call-start = ((), (), s32[]{:S(2)}) async-start(), calls=%async_computation.4 | async-start | bytes 1081344 | tf_op jit(solution)/shard_map/all_gather | solution.py:60
  592.4 308.6 %reduce-scatter.3.cloned.1.call-start = ((), (), s32[]{:S(2)}) async-start(), calls=%async_computation.5 | async-start | bytes 2162688 | tf_op jit(solution)/shard_map/reduce_scatter | solution.py:63
  687.1 248.9 %reduce-scatter.5.cloned.1.call-start = ((), (), s32[]{:S(2)}) async-start(), calls=%async_computation.6 | async-start | bytes 73728 | tf_op jit(solution)/shard_map/reduce_scatter | solution.py:64
Sparse Core Ops, SparseCore 0:
  21.7 73.3 all-gather.2
  187.0 257.4 all-reduce.2
  592.5 76.7 all-gather.4
  687.2 213.7 reduce-scatter.2
  904.0 31.8 reduce-scatter.4
where the time goes:
time: 944 us
  waiting for transfers between devices  640 us (68%)
  blocking collectives  246 us (26%)
  matrix products  35.2 us (4%)
  between operations  16.3 us (2%)
    psum x1, waiting for transfers between devices, shards(): whole_sum = lax.psum(pooled_part, ('ctx', 'cls'))  257 us
    reduce_scatter x1, waiting for transfers between devices, shards(): lax.psum_scatter(query_part, 'ctx', scatter_dimension=1, tiled=True)  200 us
    all_gather x1, waiting for transfers between devices, shards(): lax.all_gather(grad_block, 'ctx', axis=1, tiled=True)  76.7 us
    pmax x1, blocking collectives, shards(): peak = lax.pmax(local_peak, ('ctx', 'cls'))  74.6 us
    all_gather x1, waiting for transfers between devices, shards(): scores = project_add(lax.all_gather(query_block, 'ctx', axis=1, tiled=True))  72.8 us
    psum x1, blocking collectives, shards(): inner_mean = lax.psum(inner_part, 'ctx') / full_width  69.2 us
    psum x1, blocking collectives, shards(): squares, logit_raw = lax.psum((square_part, logit_part), 'ctx')  61.5 us
    reduce_scatter x1, waiting for transfers between devices, shards(): lax.psum_scatter(column_grad, 'cls', scatter_dimension=0, tiled=True)  33.2 us
  transfers between devices with their start and end apart: 5, of which 5 were waited for; matrix products, arithmetic and copies ran while one was open for 0% of the time, Pallas kernels for 0%

commit v1 on v0

--- a/solution.py
+++ b/solution.py
@@ -57,7 +57,11 @@
         jnp.bfloat16
     )
     grad_block = lax.all_gather(pooled_grad, "cls", axis=0, tiled=True)
-    projected = project_add(lax.all_gather(grad_block, "ctx", axis=1, tiled=True))
+    projected = project_add(
+        jnp.concatenate(
+            lax.all_to_all(jnp.stack([grad_block] * lax.axis_size("ctx")), "ctx", 0, 0), axis=1
+        )
+    )
     score_grad = (weights * projected).astype(jnp.bfloat16)
     query_part = jnp.dot(score_grad, tokens, preferred_element_type=jnp.float32)
     column_grad = lax.psum_scatter(query_part, "ctx", scatter_dimension=1, tiled=True)

time: 944 us -> 908 us (0.962)
  waiting for transfers between devices: 640 us -> 562 us
  blocking collectives: 246 us -> 288 us
    all_gather x1 -> x0, waiting for transfers between devices: 76.7 us -> none  [shards(): lax.all_gather(grad_block, 'ctx', axis=1, tiled=True)]
    all_to_all x0 -> x1, blocking collectives: none -> 42.4 us  [shards(): lax.all_to_all(jnp.stack([grad_block] * lax.axis_size('ctx')), 'ctx', 0, 0)]
  transfers between devices with their start and end apart: 5 -> 4, of which waited for: 5 -> 4; matrix products, arithmetic and copies ran while one was open for 0% -> 0% of each run, Pallas kernels for 0% -> 0%
where the time goes in v1:
time: 908 us; the launch traced here: 907 us
  waiting for transfers between devices  562 us (62%)
  blocking collectives  288 us (32%)
  matrix products  34.9 us (4%)
  between operations  16.3 us (2%)
    psum x1, waiting for transfers between devices, shards(): whole_sum = lax.psum(pooled_part, ('ctx', 'cls'))  257 us
    reduce_scatter x1, waiting for transfers between devices, shards(): lax.psum_scatter(query_part, 'ctx', scatter_dimension=1, tiled=True)  199 us
    pmax x1, blocking collectives, shards(): peak = lax.pmax(local_peak, ('ctx', 'cls'))  74.6 us
    all_gather x1, waiting for transfers between devices, shards(): scores = project_add(lax.all_gather(query_block, 'ctx', axis=1, tiled=True))  72.8 us
    psum x1, blocking collectives, shards(): inner_mean = lax.psum(inner_part, 'ctx') / full_width  69.2 us
    psum x1, blocking collectives, shards(): squares, logit_raw = lax.psum((square_part, logit_part), 'ctx')  61.5 us
    all_to_all x1, blocking collectives, shards(): lax.all_to_all(jnp.stack([grad_block] * lax.axis_size('ctx')), 'ctx', 0, 0)  42.4 us
    reduce_scatter x1, waiting for transfers between devices, shards(): lax.psum_scatter(column_grad, 'cls', scatter_dimension=0, tiled=True)  33.2 us
  transfers between devices with their start and end apart: 4, of which 4 were waited for; matrix products, arithmetic and copies ran while one was open for 0% of the time, Pallas kernels for 0%

profile of v1, /device:TPU:2, one launch (start us, length us, event | category | flops | bytes accessed | tf_op | source)
XLA Modules:
  0.0 907.0 jit_solution(10396538259272321970)
XLA Ops:
  7.2 14.3 %all_gather.9 = bf16[64,256]{1,0:T(8,128)(2,1)} all-gather(bf16[8,256]{1,0:T(8,128)(2,1)} %param.9), channel_id=1, replica_groups=mesh['ctx'=32,'cls'=8] {'cls'}, dimensions={0}, use_global_device_ids=true | all-gather | bytes 36864 | tf_op jit(solution)/shard_map/all_gather | solution.py:22
  22.3 72.8 %all-gather.2.cloned.1.call-done = bf16[64,8192]{1,0:T(8,128)(2,1)} async-done(((bf16[64,256]{1,0:T(8,128)(2,1)}), bf16[64,8192]{1,0:T(8,128)(2,1)}) %all-gather.2.cloned.1.call-update) | async-done | bytes 1048592 | tf_op jit(solution)/shard_map/all_gather | solution.py:23
  95.0 8.9 select_reduce_fusion
  104.0 74.6 %pmax.7 = f32[64]{0:T(128)S(1)} all-reduce(f32[64]{0:T(128)S(1)} %get-tuple-element.20), channel_id=1, replica_groups=mesh['ctx'=32,'cls'=8] {'ctx','cls'}, use_global_device_ids=true, to_apply=%region_1.2 | all-reduce | flops 64 | bytes 512 | tf_op jit(solution)/shard_map/pmax | solution.py:28
  178.7 8.2 fusion.3
  187.0 0.1 copy.14
  187.3 257.2 %all-reduce.3.cloned.1.call-done = f32[64,8192]{1,0:T(8,128)} async-done(((f32[64,8192]{1,0:T(8,128)}), f32[64,8192]{1,0:T(8,128)}) %all-reduce.3.cloned.1.call-update) | async-done | bytes 2097168 | tf_op jit(solution)/shard_map/psum | solution.py:31
  444.5 0.8 multiply_reduce_fusion.1
  445.3 0.2 fusion.11
  445.5 61.5 %all-reduce = (f32[8,64]{1,0:T(8,128)S(1)}, f32[8]{0:T(128)S(1)}) all-reduce(f32[8,64]{1,0:T(8,128)S(1)} %bitcast.37, f32[8]{0:T(128)S(1)} %get-tuple-element.16), channel_id=1, replica_groups=mesh['ctx'=32,'cls'=8] {'ctx'}, use_global_device_ids=true, to_apply=%region_5.6 | all-reduce | flops 520 | bytes 4160 | tf_op jit(solution)/shard_map/psum | solution.py:41
  507.0 0.7 divide_subtract_fusion
  507.7 0.1 fusion.18
  507.9 0.9 multiply_multiply_fusion
  508.7 69.2 %psum.39 = f32[8]{0:T(128)S(1)} all-reduce(f32[8]{0:T(128)S(1)} %get-tuple-element.15), channel_id=1, replica_groups=mesh['ctx'=32,'cls'=8] {'ctx'}, use_global_device_ids=true, to_apply=%region_9.10 | all-reduce | flops 8 | bytes 64 | tf_op jit(solution)/shard_map/psum | solution.py:55
  578.0 0.8 multiply_convert_fusion
  578.7 12.8 %all_gather.11 = bf16[64,256]{1,0:T(8,128)(2,1)S(1)} all-gather(bf16[8,256]{1,0:T(8,128)(2,1)S(1)} %multiply_convert_fusion), channel_id=1, replica_groups=mesh['ctx'=32,'cls'=8] {'cls'}, dimensions={0}, use_global_device_ids=true | all-gather | bytes 36864 | tf_op jit(solution)/shard_map/all_gather | solution.py:59
  591.7 42.4 %all_to_all.5 = bf16[32,64,256]{2,1,0:T(8,128)(2,1)S(1)} all-to-all(bf16[32,64,256]{2,1,0:T(8,128)(2,1)S(1)} %stack.2), channel_id=1, replica_groups=mesh['ctx'=32,'cls'=8] {'ctx'}, dimensions={0} | all-to-all | bytes 2097152 | tf_op jit(solution)/shard_map/all_to_all | solution.py:62
  634.2 17.4 %fusion.1 = f32[64,8192]{1,0:T(8,128)} fusion(bf16[768,8192]{1,0:T(8,128)(2,1)} %param.7, bf16[64,8192]{1,0:T(8,128)(2,1)S(1)} %bitcast.31, f32[64,768]{1,0:T(8,128)S(1)} %get-tuple-element.21, f32[64]{0:T(128)S(1)} %pmax.7, pred[768]{0:T(1024)(128)(4,1)S(1)} %add_compare_fusion), kind=kOutput, calls=%fused_computation.2 | convolution fusion | flops 1610809344 | bytes 15926272 | tf_op jit(solution)/shard_map/dot_general | solution.py:66
  651.6 13.1 %psum.38 = f32[]{:T(128)} all-reduce(f32[]{:T(128)} %get-tuple-element.19), channel_id=1, replica_groups=mesh['ctx'=32,'cls'=8] {'cls'}, use_global_device_ids=true, to_apply=%region_7.8 | all-reduce | flops 1 | bytes 8 | tf_op jit(solution)/shard_map/psum | solution.py:46
  664.7 0.7 reshape.44
  665.3 199.0 %reduce-scatter.3.cloned.1.call-done = f32[64,256]{1,0:T(8,128)} async-done(((f32[64,8192]{1,0:T(8,128)}), f32[64,256]{1,0:T(8,128)}) %reduce-scatter.3.cloned.1.call-update) | async-done | bytes 65552 | tf_op jit(solution)/shard_map/reduce_scatter | solution.py:67
  864.3 0.1 broadcast_multiply_fusion
  864.5 1.0 copy.16
  866.1 33.2 %reduce-scatter.5.cloned.1.call-done = f32[8,256]{1,0:T(8,128)} async-done(((f32[64,256]{1,0:T(8,128)}), f32[8,256]{1,0:T(8,128)}) %reduce-scatter.5.cloned.1.call-update) | async-done | bytes 8208 | tf_op jit(solution)/shard_map/reduce_scatter | solution.py:68
  (24 shorter events, 0.6 us)
Async XLA Ops:
  7.2 87.9 %all-gather.2.cloned.1.call-start = ((), (), s32[]{:S(2)}) async-start(), calls=%async_computation.3 | async-start | bytes 1081344 | tf_op jit(solution)/shard_map/all_gather | solution.py:23
  21.6 423.0 %all-reduce.3.cloned.1.call-start = ((), (), s32[]{:S(2)}) async-start(), calls=%async_computation.4 | async-start | bytes 4194304 | tf_op jit(solution)/shard_map/psum | solution.py:31
  104.0 83.0 %copy-start = (bf16[256,512]{1,0:T(8,128)(2,1)S(1)}, bf16[256,512]{1,0:T(8,128)(2,1)}, u32[]{:S(2)}) copy-start(bf16[256,512]{1,0:T(8,128)(2,1)} %param.11) | copy-start | bytes 786436
  104.0 83.1 %copy-start.3 = (s32[512]{0:T(512)S(1)}, s32[512]{0:T(512)}, u32[]{:S(2)}) copy-start(s32[512]{0:T(512)} %param.13) | copy-start | bytes 6148
  104.0 83.2 %copy-start.2 = (f32[512]{0:T(512)S(1)}, f32[512]{0:T(512)}, u32[]{:S(2)}) copy-start(f32[512]{0:T(512)} %param.12) | copy-start | bytes 6148
  104.0 340.5 %copy-start.1 = (f32[256]{0:T(256)S(1)}, f32[256]{0:T(256)}, u32[]{:S(2)}) copy-start(f32[256]{0:T(256)} %param.10) | copy-start | bytes 3076
  186.9 677.4 %reduce-scatter.3.cloned.1.call-start = ((), (), s32[]{:S(2)}) async-start(), calls=%async_computation.5 | async-start | bytes 2162688 | tf_op jit(solution)/shard_map/reduce_scatter | solution.py:67
  651.6 247.8 %reduce-scatter.5.cloned.1.call-start = ((), (), s32[]{:S(2)}) async-start(), calls=%async_computation.6 | async-start | bytes 73728 | tf_op jit(solution)/shard_map/reduce_scatter | solution.py:68
Sparse Core Ops, SparseCore 0:
  21.7 73.3 all-gather.1
  187.0 257.4 all-reduce.2
  651.7 212.5 reduce-scatter.2
  867.4 31.9 reduce-scatter.4
